TPU v7x, 32 devices: a whole 2x2x4 slice. The times are simulated.
32 devices in a mesh: blk: 4 (over y, x), tile: 8 (over z, core).
Axes of the slice: x: 2, y: 2, z: 4, core: 2. Of those that a mesh axis runs over, the one named last changes fastest.
Arguments:
- grid_feat: bfloat16 [8192, 512], P(('blk', 'tile')), may hold values from -18 to 18
- queries: bfloat16 [8192, 512], P(('blk', 'tile')), may hold values from -90 to 90
- obs_keys: bfloat16 [256, 512], P(('blk', 'tile')), may hold values from -4 to 4
- obs_values: bfloat16 [256, 512], P(('blk', 'tile')), may hold values from -6 to 6
- block_mask: int32 [64, 2], P(('blk', 'tile')), may hold values from 0 to 1, as said below
- obs_valid: int32 [2], replicated, may hold values from 2 to 128, as said below
- out_weight: bfloat16 [512, 512], replicated, may hold values from -0.25 to 0.25
- conv_weight: bfloat16 [3, 3, 512, 512], replicated, may hold values from -0.09375 to 0.09375
Outputs:
- layer_out: bfloat16 [8192, 512], P(('blk', 'tile'))
Inputs may be any that keep to these rules, and one draw needn't show every extreme that they name: `block_mask`: row t has a 1 in column t mod 2. `obs_valid`: at least one entry equals 128.
All inputs are finite; a program needn't handle non-finite values.
Results may differ from a plain program's by a relative error of at most 0.007.
Values may be sent and summed in bfloat16 or wider, within the bound.
No kernel may reach another device: no remote copies, remote signals or barrier semaphores. Data moves between devices by JAX's collectives and lax.ppermute only.
A program may use at most 64 MiB of HBM per device.

v0:
```python
import functools
import math

import jax
import jax.numpy as jnp
from jax import lax
from jax.experimental import pallas as pl
from jax.experimental.pallas import tpu as pltpu
from jax.sharding import PartitionSpec as P

HEADS = 8
OBS_BLOCK = 128
AXES = ("blk", "tile")
PAIR = 2
PARITIES = 2
MASK_ROWS = 16
NT = (((1,), (1,)), ((), ()))


def layer_kernel(
    tiles, lon, width, nblocks, rows,
    meta_ref, low_ref, high_ref, same_ref, other_ref, queries_hbm, grid_hbm, out_weight_hbm, conv_hbm,
    out_ref, queries_ref, grid_ref, out_weight_ref, conv_ref, mixed_ref, field_ref, sems,
):
    head = width // HEADS
    pair = PAIR * head
    obs = nblocks * OBS_BLOCK
    scale = head ** (-0.5) * math.log2(math.e)
    moves = [(queries_hbm, queries_ref), (out_weight_hbm, out_weight_ref), (grid_hbm, grid_ref)]
    moves += [(conv_hbm.at[lat_off], conv_ref.at[lat_off]) for lat_off in range(3)]
    copies = [
        pltpu.make_async_copy(source, target, sems.at[i]) for i, (source, target) in enumerate(moves)
    ]
    for copy in copies:
        copy.start()

    half = OBS_BLOCK // PARITIES
    key_lane = lax.broadcasted_iota(jnp.int32, (1, OBS_BLOCK), 1)
    spread = (key_lane % half) // rows * (PARITIES * rows) + key_lane % rows
    first = key_lane < half

    def row_bias(limit_of):
        parts = []
        for parity in (meta_ref[2], 1 - meta_ref[2]):
            place = spread + parity * rows
            for block in range(0, nblocks, PARITIES):
                limit = jnp.where(first, limit_of(block), limit_of(block + 1))
                parts.append(jnp.where(place < limit, 0.0, -jnp.inf))
        return jnp.concatenate(parts, axis=1)

    def own_limit(tile, block):
        allowed = meta_ref[3 + (1 + tile) * nblocks + block] > 0
        return jnp.where(allowed, meta_ref[3 + block], 0)

    def halo_limit(row, block):
        allowed = jnp.broadcast_to(row[:, block : block + 1], (1, OBS_BLOCK)) > 0.5
        return jnp.where(allowed, meta_ref[3 + block], 0)

    mask_rows = [
        ref[2 * lon : 2 * lon + MASK_ROWS, :].astype(jnp.float32)[:1] for ref in (low_ref, high_ref)
    ]
    biases = [row_bias(functools.partial(halo_limit, mask_rows[0]))]
    biases += [row_bias(functools.partial(own_limit, t)) for t in range(tiles)]
    biases += [row_bias(functools.partial(halo_limit, mask_rows[1]))]

    copies[0].wait()
    lane = lax.broadcasted_iota(jnp.int32, (obs, pair), 1)
    ones = [(lane // head == h).astype(jnp.bfloat16) for h in range(PAIR)]

    def both_parities(cols):
        parts = [ref[:, :, cols].reshape(obs // PARITIES, pair) for ref in (same_ref, other_ref)]
        return jnp.concatenate(parts, axis=0)

    for group in range(HEADS // PAIR):
        cols = slice(group * pair, (group + 1) * pair)
        keys = both_parities(cols)
        values = both_parities(slice(width + group * pair, width + (group + 1) * pair))
        key_parts = [keys * one for one in ones]
        value_parts = jnp.concatenate(
            [jnp.concatenate([values * one, one], axis=1) for one in ones], axis=0
        )
        query = jnp.concatenate(
            [low_ref[:lon, cols], queries_ref[:, cols], high_ref[:lon, cols]], axis=0
        )
        weights = []
        for part in key_parts:
            scores = lax.dot_general(query, part, NT, preferred_element_type=jnp.float32)
            pieces = []
            for t, bias in enumerate(biases):
                piece = scores[t * lon : (t + 1) * lon] * scale + bias
                top = jnp.max(piece, axis=1, keepdims=True)
                pieces.append(jnp.exp2(piece - top).astype(jnp.bfloat16))
            weights.append(jnp.concatenate(pieces, axis=0))
        both = jnp.dot(
            jnp.concatenate(weights, axis=1), value_parts, preferred_element_type=jnp.float32
        )
        mixed_ref[:, cols] = (both[:, :pair] / both[:, pair:]).astype(jnp.bfloat16)

    copies[1].wait()
    copies[2].wait()
    projected = jnp.dot(mixed_ref[...], out_weight_ref[...], preferred_element_type=jnp.float32)
    grid = jnp.concatenate(
        [low_ref[lon : 2 * lon, :], grid_ref[...], high_ref[lon : 2 * lon, :]], axis=0
    )
    hidden = (grid.astype(jnp.float32) + projected).astype(jnp.bfloat16)
    wide = hidden.astype(jnp.float32)
    normed = wide * lax.rsqrt(jnp.mean(wide * wide, axis=-1, keepdims=True) + 1e-06)
    last = (tiles + 1) * lon
    field_ref[lon:last] = normed[lon:last].astype(jnp.bfloat16)
    field_ref[:lon] = jnp.where(meta_ref[0] > 0, normed[:lon], 0.0).astype(jnp.bfloat16)
    field_ref[last:] = jnp.where(meta_ref[1] > 0, normed[last:], 0.0).astype(jnp.bfloat16)

    sums = [None, None, None]
    for lat_off in range(3):
        copies[3 + lat_off].wait()
        moved = field_ref[lat_off * lon : (lat_off + tiles) * lon, :]
        for lon_off in range(3):
            term = jnp.dot(moved, conv_ref[lat_off, lon_off], preferred_element_type=jnp.float32)
            sums[lon_off] = term if sums[lon_off] is None else sums[lon_off] + term
    for t in range(tiles):
        here = slice(t * lon, (t + 1) * lon)
        out_ref[here, :] = (
            wide[(t + 1) * lon : (t + 2) * lon]
            + pltpu.roll(sums[0][here], 1, 0)
            + sums[1][here]
            + pltpu.roll(sums[2][here], lon - 1, 0)
        ).astype(jnp.bfloat16)


def on_device(
    grid_feat, queries, obs_keys, obs_values, block_mask, obs_valid, out_weight, conv_weight
):
    q_dev, width = queries.shape
    tiles, nblocks = block_mask.shape
    lon = q_dev // tiles
    devices = lax.axis_size(AXES)
    me = lax.axis_index(AXES)
    edge = jnp.stack([me > 0, me < devices - 1]).astype(jnp.int32)
    meta = jnp.concatenate([edge, (me % PARITIES)[None], obs_valid, block_mask.reshape(-1)])

    mask_tile = jnp.pad(block_mask.astype(jnp.bfloat16), ((0, 0), (0, width - nblocks)))

    def packed(tile):
        rows = slice(tile * lon, (tile + 1) * lon)
        mask = jnp.broadcast_to(mask_tile[tile : tile + 1], (MASK_ROWS, width))
        return jnp.concatenate([queries[rows], grid_feat[rows], mask], axis=0)

    forward = [(i, i + 1) for i in range(devices - 1)]
    backward = [(i + 1, i) for i in range(devices - 1)]
    low = lax.ppermute(packed(tiles - 1), AXES, forward)
    high = lax.ppermute(packed(0), AXES, backward)

    kv_local = jnp.concatenate([obs_keys, obs_values], axis=1)
    groups = [list(range(parity, devices, PARITIES)) for parity in range(PARITIES)]
    blocks = jnp.broadcast_to(kv_local[None], (devices // PARITIES,) + kv_local.shape)
    same = lax.all_to_all(blocks, AXES, 0, 0, axis_index_groups=groups)
    other = lax.ppermute(same, AXES, [(i, i ^ 1) for i in range(devices)])

    vmem = pl.BlockSpec(memory_space=pltpu.VMEM)
    smem = pl.BlockSpec(memory_space=pltpu.SMEM)
    flops = 2 * q_dev * width * (9 * width + 2 * width + 4 * nblocks * OBS_BLOCK)
    return pl.pallas_call(
        functools.partial(layer_kernel, tiles, lon, width, nblocks, obs_keys.shape[0]),
        out_shape=jax.ShapeDtypeStruct((q_dev, width), jnp.bfloat16),
        in_specs=[smem] + [vmem] * 4 + [pl.BlockSpec(memory_space=pltpu.HBM)] * 4,
        out_specs=vmem,
        scratch_shapes=[
            pltpu.VMEM(queries.shape, jnp.bfloat16),
            pltpu.VMEM(grid_feat.shape, jnp.bfloat16),
            pltpu.VMEM(out_weight.shape, jnp.bfloat16),
            pltpu.VMEM(conv_weight.shape, jnp.bfloat16),
            pltpu.VMEM(((tiles + 2) * lon, width), jnp.bfloat16),
            pltpu.VMEM(((tiles + 2) * lon, width), jnp.bfloat16),
            pltpu.SemaphoreType.DMA((6,)),
        ],
        compiler_params=pltpu.CompilerParams(vmem_limit_bytes=48 * 2**20),
        cost_estimate=pl.CostEstimate(
            flops=flops, bytes_accessed=2 * conv_weight.size, transcendentals=0
        ),
        name="layer",
    )(meta, low, high, same, other, queries, grid_feat, out_weight, conv_weight)


def solution(mesh):
    in_specs = (
        P(AXES, None),
        P(AXES, None),
        P(AXES, None),
        P(AXES, None),
        P(AXES, None),
        P(),
        P(),
        P(),
    )
    return jax.shard_map(
        on_device, mesh=mesh, in_specs=in_specs, out_specs=P(AXES, None), check_vma=False
    )
```

profile of v0, /device:TPU:4, one launch (start us, length us, event | category | flops | bytes accessed | tf_op | source)
XLA Modules:
  0.0 35.8 jit_solution(5153436888746409472)
XLA Ops:
  0.0 0.7 %pad_maximum_fusion.2 = bf16[8,1024]{1,0:T(8,128)(2,1)S(1)} fusion(bf16[8,512]{1,0:T(8,128)(2,1)} %param.11, bf16[8,512]{1,0:T(8,128)(2,1)} %param.10), kind=kLoop, calls=%fused_computation.2 | loop fusion | flops 32768 | bytes 32768 | tf_op jit(solution)/shard_map/concatenate | solution.py:153
  0.7 0.7 %broadcast_in_dim.28 = bf16[16,8,1024]{2,1,0:T(8,128)(2,1)} broadcast(bf16[8,1024]{1,0:T(8,128)(2,1)S(1)} %pad_maximum_fusion.2), dimensions={1,2} | broadcast | bytes 278528 | tf_op jit(solution)/shard_map/broadcast_in_dim | solution.py:155
  1.5 7.3 %all-to-all-start = ((bf16[16,8,1024]{2,1,0:T(8,128)(2,1)}), bf16[16,8,1024]{2,1,0:T(8,128)(2,1)S(1)}, u32[]{:S(2)}, u32[]{:S(2)}) async-start(bf16[16,8,1024]{2,1,0:T(8,128)(2,1)} %broadcast_in_dim.28), calls=%async_computation | async-start | bytes 524288 | tf_op jit(solution)/shard_map/all_to_all | solution.py:156
  8.7 0.7 %convert_element_type.9 = bf16[2,2]{1,0:T(2,128)(2,1)S(1)} convert(s32[2,2]{1,0:T(2,128)} %param.12) | non-fusion elementwise | flops 4 | bytes 24 | tf_op jit(solution)/shard_map/convert_element_type | solution.py:141
  9.4 1.1 %fusion = (bf16[128,512]{1,0:T(8,128)(2,1)S(1)}, bf16[128,512]{1,0:T(8,128)(2,1)S(1)}, bf16[128,512]{1,0:T(8,128)(2,1)S(1)}, bf16[128,512]{1,0:T(8,128)(2,1)S(1)}) fusion(bf16[256,512]{1,0:T(8,128)(2,1)} %queries_hbm.1, bf16[256,512]{1,0:T(8,128)(2,1)} %grid_hbm.1), kind=kLoop, calls=%fused_computation.7 | loop fusion | bytes 1048576 | tf_op jit(solution)/shard_map/slice | solution.py:146
  10.6 4.9 %collective-permute-start.1 = (bf16[272,512]{1,0:T(8,128)(2,1)S(1)}, bf16[272,512]{1,0:T(8,128)(2,1)S(1)}, u32[]{:S(2)}, u32[]{:S(2)}) collective-permute-start(bf16[272,512]{1,0:T(8,128)(2,1)S(1)} %pad_maximum_fusion.1), channel_id=1, source_target_pairs={{1,0},{2,1},{3,2},{4,3},{5,4},{6,5},{7,6},{8,7},{9,8},{10,9},{11,1... | collective-permute-start | bytes 835592 | tf_op jit(solution)/shard_map/ppermute | solution.py:151
  15.6 1.9 %collective-permute-start = (bf16[272,512]{1,0:T(8,128)(2,1)S(1)}, bf16[272,512]{1,0:T(8,128)(2,1)S(1)}, u32[]{:S(2)}, u32[]{:S(2)}) collective-permute-start(bf16[272,512]{1,0:T(8,128)(2,1)S(1)} %pad_maximum_fusion), channel_id=1, source_target_pairs={{0,1},{1,2},{2,3},{3,4},{4,5},{5,6},{6,7},{7,8},{8,9},{9,10},{10,1... | collective-permute-start | bytes 835592 | tf_op jit(solution)/shard_map/ppermute | solution.py:150
  17.5 0.5 %all-to-all-done.same_ref = bf16[16,8,1024]{2,1,0:T(8,128)(2,1)S(1)} async-done(((bf16[16,8,1024]{2,1,0:T(8,128)(2,1)}), bf16[16,8,1024]{2,1,0:T(8,128)(2,1)S(1)}, u32[]{:S(2)}, u32[]{:S(2)}) %all-to-all-start) | async-done | bytes 262176 | tf_op jit(solution)/shard_map/all_to_all | solution.py:156
  18.0 0.0 collective-permute-start.2
  18.0 0.8 %reshape.4 = s32[4]{0:T(128)S(1)} reshape(s32[2,2]{1,0:T(2,128)} %param.12) | data formatting | bytes 32 | tf_op jit(solution)/shard_map/reshape | solution.py:139
  18.8 0.1 add_convert_fusion
  18.9 0.7 %pad_add_fusion.meta_ref = s32[9]{0:T(128)S(1)} fusion(s32[4]{0:T(128)S(1)} %reshape.4, s32[2]{0:T(128)} %param.13, s32[1]{0:T(128)} %bitcast.2, s32[2]{0:T(128)S(1)} %add_convert_fusion), kind=kLoop, calls=%fused_computation.6 | loop fusion | flops 27 | bytes 72 | tf_op jit(solution)/shard_map/concatenate | solution.py:139
  19.6 2.8 %collective-permute-done.1.high_ref = bf16[272,512]{1,0:T(8,128)(2,1)S(1)} collective-permute-done((bf16[272,512]{1,0:T(8,128)(2,1)S(1)}, bf16[272,512]{1,0:T(8,128)(2,1)S(1)}, u32[]{:S(2)}, u32[]{:S(2)}) %collective-permute-start.1) | collective-permute-done | bytes 278560 | tf_op jit(solution)/shard_map/ppermute | solution.py:151
  22.4 4.7 %collective-permute-done.low_ref = bf16[272,512]{1,0:T(8,128)(2,1)S(1)} collective-permute-done((bf16[272,512]{1,0:T(8,128)(2,1)S(1)}, bf16[272,512]{1,0:T(8,128)(2,1)S(1)}, u32[]{:S(2)}, u32[]{:S(2)}) %collective-permute-start) | collective-permute-done | bytes 278560 | tf_op jit(solution)/shard_map/ppermute | solution.py:150
  27.1 0.0 collective-permute-done.2.other_ref
  27.1 0.0 copy-start
  27.1 0.9 %copy-done = bf16[256,512]{1,0:T(8,128)(2,1)S(1)} copy-done((bf16[256,512]{1,0:T(8,128)(2,1)S(1)}, bf16[256,512]{1,0:T(8,128)(2,1)}, u32[]{:S(2)}) %copy-start) | copy-done | bytes 262168
  28.0 0.0 copy-start.1
  28.0 0.9 %copy-done.1 = bf16[256,512]{1,0:T(8,128)(2,1)S(1)} copy-done((bf16[256,512]{1,0:T(8,128)(2,1)S(1)}, bf16[256,512]{1,0:T(8,128)(2,1)}, u32[]{:S(2)}) %copy-start.1) | copy-done | bytes 262168
  29.0 0.0 copy-start.2
  29.0 1.0 %copy-done.2 = bf16[512,512]{1,0:T(8,128)(2,1)S(1)} copy-done((bf16[512,512]{1,0:T(8,128)(2,1)S(1)}, bf16[512,512]{1,0:T(8,128)(2,1)}, u32[]{:S(2)}) %copy-start.2) | copy-done | bytes 524312
  30.0 5.8 %layer.1 = bf16[256,512]{1,0:T(8,128)(2,1)} custom-call(s32[9]{0:T(128)S(1)} %pad_add_fusion.meta_ref, bf16[272,512]{1,0:T(8,128)(2,1)S(1)} %collective-permute-done.low_ref, bf16[272,512]{1,0:T(8,128)(2,1)S(1)} %collective-permute-done.1.high_ref, bf16[16,8,1024]{2,1,0:T(8,128)(2,1)S(1)} %all-to-all-done.same_ref, ...), custom_call_target="tpu_custom_call" | custom-call | flops 1744830464 | bytes 4718592 | tf_op jit(solution)/shard_map/layer/pallas_call | solution.py:162
  (5 shorter events, 0.1 us)
Async XLA Ops:
  1.5 16.6 %all-to-all-start = ((bf16[16,8,1024]{2,1,0:T(8,128)(2,1)}), bf16[16,8,1024]{2,1,0:T(8,128)(2,1)S(1)}, u32[]{:S(2)}, u32[]{:S(2)}) async-start(bf16[16,8,1024]{2,1,0:T(8,128)(2,1)} %broadcast_in_dim.28), calls=%async_computation | async-start | bytes 524288 | tf_op jit(solution)/shard_map/all_to_all | solution.py:156
  10.6 11.8 %collective-permute-start.1 = (bf16[272,512]{1,0:T(8,128)(2,1)S(1)}, bf16[272,512]{1,0:T(8,128)(2,1)S(1)}, u32[]{:S(2)}, u32[]{:S(2)}) collective-permute-start(bf16[272,512]{1,0:T(8,128)(2,1)S(1)} %pad_maximum_fusion.1), channel_id=1, source_target_pairs={{1,0},{2,1},{3,2},{4,3},{5,4},{6,5},{7,6},{8,7},{9,8},{10,9},{11,1... | collective-permute-start | bytes 835592 | tf_op jit(solution)/shard_map/ppermute | solution.py:151
  15.6 11.5 %collective-permute-start = (bf16[272,512]{1,0:T(8,128)(2,1)S(1)}, bf16[272,512]{1,0:T(8,128)(2,1)S(1)}, u32[]{:S(2)}, u32[]{:S(2)}) collective-permute-start(bf16[272,512]{1,0:T(8,128)(2,1)S(1)} %pad_maximum_fusion), channel_id=1, source_target_pairs={{0,1},{1,2},{2,3},{3,4},{4,5},{5,6},{6,7},{7,8},{8,9},{9,10},{10,1... | collective-permute-start | bytes 835592 | tf_op jit(solution)/shard_map/ppermute | solution.py:150
  18.0 9.0 %collective-permute-start.2 = (bf16[16,8,1024]{2,1,0:T(8,128)(2,1)S(1)}, bf16[16,8,1024]{2,1,0:T(8,128)(2,1)S(1)}, u32[]{:S(2)}, u32[]{:S(2)}) collective-permute-start(bf16[16,8,1024]{2,1,0:T(8,128)(2,1)S(1)} %all-to-all-done.same_ref), channel_id=1, source_target_pairs={{0,1},{1,0},{2,3},{3,2},{4,5},{5,4},{6,7},{7,6},{8,9},{9,8},{10,11... | collective-permute-start | bytes 786440 | tf_op jit(solution)/shard_map/ppermute | solution.py:157
  27.1 1.0 %copy-start = (bf16[256,512]{1,0:T(8,128)(2,1)S(1)}, bf16[256,512]{1,0:T(8,128)(2,1)}, u32[]{:S(2)}) copy-start(bf16[256,512]{1,0:T(8,128)(2,1)} %queries_hbm.1) | copy-start | bytes 786436
  28.0 0.9 %copy-start.1 = (bf16[256,512]{1,0:T(8,128)(2,1)S(1)}, bf16[256,512]{1,0:T(8,128)(2,1)}, u32[]{:S(2)}) copy-start(bf16[256,512]{1,0:T(8,128)(2,1)} %grid_hbm.1) | copy-start | bytes 786436
  29.0 1.0 %copy-start.2 = (bf16[512,512]{1,0:T(8,128)(2,1)S(1)}, bf16[512,512]{1,0:T(8,128)(2,1)}, u32[]{:S(2)}) copy-start(bf16[512,512]{1,0:T(8,128)(2,1)} %out_weight_hbm.1) | copy-start | bytes 1572868
where the time goes:
time: 36.2 us; the launch traced here: 35.8 us
  starting transfers between devices  14.2 us (39%)
  waiting for transfers between devices  7.97 us (22%)
  Pallas kernels  5.75 us (16%)
  local copies, waits for them, and re-layouts  5.6 us (15%)
  other arithmetic  2.25 us (6%)
    all_to_all x1, starting transfers between devices, on_device(): same = lax.all_to_all(blocks, AXES, 0, 0, axis_index_groups=groups)  7.28 us
    pallas_call x1, Pallas kernels, on_device(): pl.pallas_call(functools.partial(layer_kernel, tiles, lon, width, nblocks...  5.75 us
    ppermute x1, starting transfers between devices, on_device(): high = lax.ppermute(packed(0), AXES, backward)  4.95 us
    ppermute x1, waiting for transfers between devices, on_device(): low = lax.ppermute(packed(tiles - 1), AXES, forward)  4.66 us
    unnamed x6, local copies, waits for them, and re-layouts  2.94 us
    ppermute x1, waiting for transfers between devices, on_device(): high = lax.ppermute(packed(0), AXES, backward)  2.81 us
    ppermute x1, starting transfers between devices, on_device(): low = lax.ppermute(packed(tiles - 1), AXES, forward)  1.92 us
    slice x1, local copies, waits for them, and re-layouts, packed(): return jnp.concatenate([queries[rows], grid_feat[rows], mask], axis=0)  1.13 us
  transfers between devices with their start and end apart: 4, of which 3 were waited for; matrix products, arithmetic and copies ran while one was open for 10% of the time, Pallas kernels for 0%

commit v1 on v0

v1 whole, which is shorter than its diff:
```python
import functools
import math

import jax
import jax.numpy as jnp
from jax import lax
from jax.experimental import pallas as pl
from jax.experimental.pallas import tpu as pltpu
from jax.sharding import PartitionSpec as P

HEADS = 8
OBS_BLOCK = 128
AXES = ("blk", "tile")
PAIR = 2
CORES = 2
MASK_LANES = 128
NT = (((1,), (1,)), ((), ()))


def layer_kernel(
    tiles, lon, width, nblocks, rows,
    meta_ref, near_ref, far_ref, same_ref, other_ref, *refs,
):
    queries_refs, grid_refs = refs[:tiles], refs[tiles : 2 * tiles]
    out_weight_refs = refs[2 * tiles : 2 * tiles + 2]
    conv_hbm, out_ref, conv_ref, mixed_ref, field_ref, sems = refs[2 * tiles + 2 :]
    head = width // HEADS
    pair = PAIR * head
    obs = nblocks * OBS_BLOCK
    scale = head ** (-0.5) * math.log2(math.e)
    moves = [(conv_hbm.at[lat_off], conv_ref.at[lat_off]) for lat_off in range(3)]
    copies = [
        pltpu.make_async_copy(source, target, sems.at[i]) for i, (source, target) in enumerate(moves)
    ]
    for copy in copies:
        copy.start()

    core, near_pair, far_pair, far_exists = (meta_ref[i] for i in range(4))
    half = OBS_BLOCK // CORES
    key_lane = lax.broadcasted_iota(jnp.int32, (1, OBS_BLOCK), 1)
    spread = (key_lane % half) // rows * (CORES * rows) + key_lane % rows
    first = key_lane < half

    def row_bias(limit_of):
        parts = []
        for parity in (core, 1 - core):
            place = spread + parity * rows
            for block in range(0, nblocks, CORES):
                limit = jnp.where(first, limit_of(block), limit_of(block + 1))
                parts.append(jnp.where(place < limit, 0.0, -jnp.inf))
        return jnp.concatenate(parts, axis=1)

    def own_limit(tile, block):
        allowed = meta_ref[4 + (1 + tile) * nblocks + block] > 0
        return jnp.where(allowed, meta_ref[4 + block], 0)

    def halo_limit(row, block):
        allowed = jnp.broadcast_to(row[:, block : block + 1], (1, OBS_BLOCK)) > 0.5
        return jnp.where(allowed, meta_ref[4 + block], 0)

    def mask_row(index, take_first):
        block = other_ref[index][:, 2 * width :].astype(jnp.float32)
        return jnp.where(take_first, block[:1], block[tiles - 1 : tiles])

    biases = [row_bias(functools.partial(halo_limit, mask_row(near_pair, core == 0)))]
    biases += [row_bias(functools.partial(own_limit, t)) for t in range(tiles)]
    biases += [row_bias(functools.partial(halo_limit, mask_row(far_pair, core == 1)))]

    lane = lax.broadcasted_iota(jnp.int32, (obs, pair), 1)
    ones = [(lane // head == h).astype(jnp.bfloat16) for h in range(PAIR)]

    def both_cores(cols):
        parts = [ref[:, :, cols].reshape(obs // CORES, pair) for ref in (same_ref, other_ref)]
        return jnp.concatenate(parts, axis=0)

    for group in range(HEADS // PAIR):
        cols = slice(group * pair, (group + 1) * pair)
        keys = both_cores(cols)
        values = both_cores(slice(width + group * pair, width + (group + 1) * pair))
        key_parts = [keys * one for one in ones]
        value_parts = jnp.concatenate(
            [jnp.concatenate([values * one, one], axis=1) for one in ones], axis=0
        )
        query = jnp.concatenate(
            [near_ref[:lon, cols]] + [ref[:, cols] for ref in queries_refs] + [far_ref[:lon, cols]],
            axis=0,
        )
        weights = []
        for part in key_parts:
            scores = lax.dot_general(query, part, NT, preferred_element_type=jnp.float32)
            pieces = []
            for t, bias in enumerate(biases):
                piece = scores[t * lon : (t + 1) * lon] * scale + bias
                top = jnp.max(piece, axis=1, keepdims=True)
                pieces.append(jnp.exp2(piece - top).astype(jnp.bfloat16))
            weights.append(jnp.concatenate(pieces, axis=0))
        both = jnp.dot(
            jnp.concatenate(weights, axis=1), value_parts, preferred_element_type=jnp.float32
        )
        mixed_ref[:, cols] = (both[:, :pair] / both[:, pair:]).astype(jnp.bfloat16)

    out_weight = jnp.concatenate([ref[...] for ref in out_weight_refs], axis=0)
    projected = jnp.dot(mixed_ref[...], out_weight, preferred_element_type=jnp.float32)
    grid = jnp.concatenate(
        [near_ref[lon:, :]] + [ref[...] for ref in grid_refs] + [far_ref[lon:, :]], axis=0
    )
    hidden = (grid.astype(jnp.float32) + projected).astype(jnp.bfloat16)
    wide = hidden.astype(jnp.float32)
    normed = wide * lax.rsqrt(jnp.mean(wide * wide, axis=-1, keepdims=True) + 1e-06)
    last = (tiles + 1) * lon
    near_place = pl.multiple_of((1 - core) * last, lon)
    far_place = pl.multiple_of(core * last, lon)
    field_ref[lon:last] = normed[lon:last].astype(jnp.bfloat16)
    field_ref[pl.ds(near_place, lon)] = normed[:lon].astype(jnp.bfloat16)
    field_ref[pl.ds(far_place, lon)] = jnp.where(far_exists > 0, normed[last:], 0.0).astype(
        jnp.bfloat16
    )

    sums = [None, None, None]
    for lat_off in range(3):
        copies[lat_off].wait()
        moved = field_ref[lat_off * lon : (lat_off + tiles) * lon, :]
        for lon_off in range(3):
            term = jnp.dot(moved, conv_ref[lat_off, lon_off], preferred_element_type=jnp.float32)
            sums[lon_off] = term if sums[lon_off] is None else sums[lon_off] + term
    for t in range(tiles):
        here = slice(t * lon, (t + 1) * lon)
        out_ref[here, :] = (
            wide[(t + 1) * lon : (t + 2) * lon]
            + pltpu.roll(sums[0][here], 1, 0)
            + sums[1][here]
            + pltpu.roll(sums[2][here], lon - 1, 0)
        ).astype(jnp.bfloat16)


def on_device(
    grid_feat, queries, obs_keys, obs_values, block_mask, obs_valid, out_weight, conv_weight
):
    q_dev, width = queries.shape
    tiles, nblocks = block_mask.shape
    rows = obs_keys.shape[0]
    lon = q_dev // tiles
    blks, chain = lax.axis_size("blk"), lax.axis_size("tile")
    devices = blks * chain
    pairs = devices // CORES
    me = lax.axis_index(AXES)
    core = me % CORES

    mask_block = jnp.pad(
        block_mask.astype(jnp.bfloat16), ((0, rows - tiles), (0, MASK_LANES - nblocks))
    )
    block = jnp.concatenate([obs_keys, obs_values, mask_block], axis=1)
    members = chain // CORES
    groups = [
        [b * chain + i * CORES + c for i in range(members)] for b in range(blks) for c in range(CORES)
    ]
    column = lax.all_to_all(
        jnp.broadcast_to(block[None], (members,) + block.shape), AXES, 0, 0, axis_index_groups=groups
    )

    def pieces(array, count):
        return jnp.split(array, count, axis=0)

    query_rows, grid_rows, weight_rows = lax.optimization_barrier(
        (pieces(queries, tiles), pieces(grid_feat, tiles), pieces(out_weight, 2))
    )
    first = jnp.concatenate([query_rows[0], grid_rows[0]], axis=0)
    last = jnp.concatenate([query_rows[-1], grid_rows[-1]], axis=0)
    across = [(i, i + 1) for i in range(1, devices - 1, CORES)]
    across += [(target, source) for source, target in across]
    swap = [(i, i ^ 1) for i in range(devices)]
    far = lax.ppermute(jnp.where(core == 0, first, last), AXES, across)
    near = lax.ppermute(jnp.where(core == 0, last, first), AXES, swap)

    same = lax.all_to_all(
        jnp.broadcast_to(column[None], (blks,) + column.shape), "blk", 0, 0
    ).reshape((pairs,) + block.shape)
    other = lax.ppermute(same, AXES, swap)

    near_pair = me // CORES
    far_pair = near_pair + 2 * core - 1
    far_exists = (far_pair >= 0) & (far_pair < pairs)
    scalars = [core, near_pair, jnp.clip(far_pair, 0, pairs - 1), far_exists]
    meta = jnp.concatenate(
        [jnp.stack([s.astype(jnp.int32) for s in scalars]), obs_valid, block_mask.reshape(-1)]
    )

    vmem = pl.BlockSpec(memory_space=pltpu.VMEM)
    smem = pl.BlockSpec(memory_space=pltpu.SMEM)
    hbm = pl.BlockSpec(memory_space=pltpu.HBM)
    flops = 2 * q_dev * width * (9 * width + 2 * width + 4 * nblocks * OBS_BLOCK)
    return pl.pallas_call(
        functools.partial(layer_kernel, tiles, lon, width, nblocks, rows),
        out_shape=jax.ShapeDtypeStruct((q_dev, width), jnp.bfloat16),
        in_specs=[smem] + [vmem] * (6 + 2 * tiles) + [hbm],
        out_specs=vmem,
        scratch_shapes=[
            pltpu.VMEM(conv_weight.shape, jnp.bfloat16),
            pltpu.VMEM(((tiles + 2) * lon, width), jnp.bfloat16),
            pltpu.VMEM(((tiles + 2) * lon, width), jnp.bfloat16),
            pltpu.SemaphoreType.DMA((3,)),
        ],
        compiler_params=pltpu.CompilerParams(vmem_limit_bytes=48 * 2**20),
        cost_estimate=pl.CostEstimate(
            flops=flops, bytes_accessed=2 * conv_weight.size, transcendentals=0
        ),
        name="layer",
    )(meta, near, far, same, other, *query_rows, *grid_rows, *weight_rows, conv_weight)


def solution(mesh):
    in_specs = (
        P(AXES, None),
        P(AXES, None),
        P(AXES, None),
        P(AXES, None),
        P(AXES, None),
        P(),
        P(),
        P(),
    )
    return jax.shard_map(
        on_device, mesh=mesh, in_specs=in_specs, out_specs=P(AXES, None), check_vma=False
    )
```

time: 36.2 us -> 42 us (1.16)
  waiting for transfers between devices: 7.97 us -> 16.8 us
  local copies, waits for them, and re-layouts: 5.6 us -> 3.78 us
  starting transfers between devices: 14.2 us -> 12.9 us
  Pallas kernels: 5.75 us -> 6.59 us
  other arithmetic: 2.25 us -> 1.52 us
    all_to_all x1 -> x2, waiting for transfers between devices: 0.5 us -> 8.28 us  [the longest x1 4.76 us: on_device(): lax.all_to_all(jnp.broadcast_to(column[None], (blks,) + column.shape), 'b...]
    ppermute x3, starting transfers between devices: 6.87 us -> 3.79 us  [the longest x1 3.22 us: on_device(): far = lax.ppermute(jnp.where(core == 0, first, last), AXES, across)]
    unnamed x6, local copies, waits for them, and re-layouts: 2.94 us -> 0.03 us
    split x0 -> x2, local copies, waits for them, and re-layouts: none -> 2.2 us  [pieces(): return jnp.split(array, count, axis=0)]
    all_to_all x1 -> x2, starting transfers between devices: 7.28 us -> 9.09 us  [the longest x1 4.87 us: on_device(): lax.all_to_all(jnp.broadcast_to(block[None], (members,) + block.shape), A...]
    slice x2 -> x0, local copies, waits for them, and re-layouts: 1.16 us -> none  [the longest x1 1.13 us: packed(): return jnp.concatenate([queries[rows], grid_feat[rows], mask], axis=0)]
    ppermute x3, waiting for transfers between devices: 7.47 us -> 8.47 us  [the longest x1 8.47 us: on_device(): far = lax.ppermute(jnp.where(core == 0, first, last), AXES, across)]
    pallas_call x1, Pallas kernels: 5.75 us -> 6.59 us  [on_device(): pl.pallas_call(functools.partial(layer_kernel, tiles, lon, width, nblocks...]
  transfers between devices with their start and end apart: 4 -> 5, of which waited for: 3 -> 3; matrix products, arithmetic and copies ran while one was open for 10% -> 6% of each run, Pallas kernels for 0% -> 0%
where the time goes in v1:
time: 42 us; the launch traced here: 41.6 us
  waiting for transfers between devices  16.8 us (40%)
  starting transfers between devices  12.9 us (31%)
  Pallas kernels  6.59 us (16%)
  local copies, waits for them, and re-layouts  3.78 us (9%)
  other arithmetic  1.52 us (4%)
    ppermute x1, waiting for transfers between devices, on_device(): far = lax.ppermute(jnp.where(core == 0, first, last), AXES, across)  8.47 us
    pallas_call x1, Pallas kernels, on_device(): pl.pallas_call(functools.partial(layer_kernel, tiles, lon, width, nblocks...  6.59 us
    all_to_all x1, starting transfers between devices, on_device(): lax.all_to_all(jnp.broadcast_to(block[None], (members,) + block.shape), A...  4.87 us
    all_to_all x1, waiting for transfers between devices, on_device(): lax.all_to_all(jnp.broadcast_to(column[None], (blks,) + column.shape), 'b...  4.76 us
    all_to_all x1, starting transfers between devices, on_device(): lax.all_to_all(jnp.broadcast_to(column[None], (blks,) + column.shape), 'b...  4.22 us
    all_to_all x1, waiting for transfers between devices, on_device(): lax.all_to_all(jnp.broadcast_to(block[None], (members,) + block.shape), A...  3.53 us
    ppermute x1, starting transfers between devices, on_device(): far = lax.ppermute(jnp.where(core == 0, first, last), AXES, across)  3.22 us
    split x2, local copies, waits for them, and re-layouts, pieces(): return jnp.split(array, count, axis=0)  2.2 us
  transfers between devices with their start and end apart: 5, of which 3 were waited for; matrix products, arithmetic and copies ran while one was open for 6% of the time, Pallas kernels for 0%

profile of v1, /device:TPU:4, one launch (start us, length us, event | category | flops | bytes accessed | tf_op | source)
XLA Modules:
  0.0 41.6 jit_solution(5919887822558508186)
XLA Ops:
  0.0 0.0 copy-start.1
  0.0 0.0 copy-start
  0.0 0.8 %convert_element_type.6 = bf16[2,2]{1,0:T(2,128)(2,1)S(1)} convert(s32[2,2]{1,0:T(2,128)} %param.12) | non-fusion elementwise | flops 4 | bytes 24 | tf_op jit(solution)/shard_map/convert_element_type | solution.py:150
  0.8 0.7 %fusion.1 = bf16[8,1152]{1,0:T(8,128)(2,1)S(1)} fusion(bf16[2,2]{1,0:T(2,128)(2,1)S(1)} %convert_element_type.6, bf16[8,512]{1,0:T(8,128)(2,1)} %param.11, bf16[8,512]{1,0:T(8,128)(2,1)} %param.10), kind=kLoop, calls=%fused_computation.4 | loop fusion | flops 73728 | bytes 34824 | tf_op jit(solution)/shard_map/concatenate | solution.py:152
  1.5 0.6 %broadcast_in_dim.4 = bf16[4,8,1152]{2,1,0:T(8,128)(2,1)} broadcast(bf16[8,1152]{1,0:T(8,128)(2,1)S(1)} %fusion.1), dimensions={1,2} | broadcast | bytes 92160 | tf_op jit(solution)/shard_map/broadcast_in_dim | solution.py:158
  2.1 4.9 %all-to-all-start = ((bf16[4,8,1152]{2,1,0:T(8,128)(2,1)}), bf16[4,8,1152]{2,1,0:T(8,128)(2,1)S(1)}, u32[]{:S(2)}, u32[]{:S(2)}) async-start(bf16[4,8,1152]{2,1,0:T(8,128)(2,1)} %broadcast_in_dim.4), calls=%async_computation | async-start | bytes 147456 | tf_op jit(solution)/shard_map/all_to_all | solution.py:157
  7.0 1.1 %fusion.2 = (bf16[256,512]{1,0:T(8,128)(2,1)S(1)}, bf16[256,512]{1,0:T(8,128)(2,1)S(1)}) fusion(bf16[512,512]{1,0:T(8,128)(2,1)} %param.14), kind=kLoop, calls=%fused_computation.9 | loop fusion | bytes 1048576 | tf_op jit(solution)/shard_map/split | solution.py:162
  8.1 1.1 %fusion.3 = (bf16[128,512]{1,0:T(8,128)(2,1)S(1)}, bf16[128,512]{1,0:T(8,128)(2,1)S(1)}, bf16[128,512]{1,0:T(8,128)(2,1)S(1)}, bf16[128,512]{1,0:T(8,128)(2,1)S(1)}) fusion(bf16[256,512]{1,0:T(8,128)(2,1)} %param.8, bf16[256,512]{1,0:T(8,128)(2,1)} %param.9), kind=kLoop, calls=%fused_computation.10 | loop fusion | bytes 1048576 | tf_op jit(solution)/shard_map/split | solution.py:162
  9.2 3.5 %all-to-all-done = bf16[4,8,1152]{2,1,0:T(8,128)(2,1)S(1)} async-done(((bf16[4,8,1152]{2,1,0:T(8,128)(2,1)}), bf16[4,8,1152]{2,1,0:T(8,128)(2,1)S(1)}, u32[]{:S(2)}, u32[]{:S(2)}) %all-to-all-start) | async-done | bytes 73760 | tf_op jit(solution)/shard_map/all_to_all | solution.py:157
  12.8 0.7 %broadcast_in_dim.5 = bf16[4,4,8,1152]{3,2,1,0:T(8,128)(2,1)} broadcast(bf16[4,8,1152]{2,1,0:T(8,128)(2,1)S(1)} %all-to-all-done), dimensions={1,2,3} | broadcast | bytes 368640 | tf_op jit(solution)/shard_map/broadcast_in_dim | solution.py:176
  13.5 4.2 %all-to-all-start.1 = ((bf16[4,4,8,1152]{3,2,1,0:T(8,128)(2,1)}), bf16[4,4,8,1152]{3,2,1,0:T(8,128)(2,1)S(1)}, u32[]{:S(2)}, u32[]{:S(2)}) async-start(bf16[4,4,8,1152]{3,2,1,0:T(8,128)(2,1)} %broadcast_in_dim.5), calls=%async_computation.1 | async-start | bytes 589824 | tf_op jit(solution)/shard_map/all_to_all | solution.py:175
  17.7 4.8 %all-to-all-done.1 = bf16[4,4,8,1152]{3,2,1,0:T(8,128)(2,1)S(1)} async-done(((bf16[4,4,8,1152]{3,2,1,0:T(8,128)(2,1)}), bf16[4,4,8,1152]{3,2,1,0:T(8,128)(2,1)S(1)}, u32[]{:S(2)}, u32[]{:S(2)}) %all-to-all-start.1) | async-done | bytes 294944 | tf_op jit(solution)/shard_map/all_to_all | solution.py:175
  22.5 0.0 collective-permute-start.2
  22.5 0.6 %collective-permute-start = (bf16[256,512]{1,0:T(8,128)(2,1)S(1)}, bf16[256,512]{1,0:T(8,128)(2,1)S(1)}, u32[]{:S(2)}, u32[]{:S(2)}) collective-permute-start(bf16[256,512]{1,0:T(8,128)(2,1)S(1)} %get-tuple-element.18), channel_id=1, source_target_pairs={{0,1},{1,0},{2,3},{3,2},{4,5},{5,4},{6,7},{7,6},{8,9},{9,8},{10,11... | collective-permute-start | bytes 786440 | tf_op jit(solution)/shard_map/ppermute | solution.py:173
  23.1 3.2 %collective-permute-start.1 = (bf16[256,512]{1,0:T(8,128)(2,1)S(1)}, bf16[256,512]{1,0:T(8,128)(2,1)S(1)}, u32[]{:S(2)}, u32[]{:S(2)}) collective-permute-start(bf16[256,512]{1,0:T(8,128)(2,1)S(1)} %get-tuple-element.17), channel_id=1, source_target_pairs={{1,2},{3,4},{5,6},{7,8},{9,10},{11,12},{13,14},{15,16},{17,18},{19... | collective-permute-start | bytes 786440 | tf_op jit(solution)/shard_map/ppermute | solution.py:172
  26.4 0.0 copy-done.1
  26.4 0.1 reshape.8
  26.5 0.0 copy-done
  26.5 0.1 concatenate.12.meta_ref
  26.5 0.0 collective-permute-done.near_ref
  26.6 8.5 %collective-permute-done.1.far_ref = bf16[256,512]{1,0:T(8,128)(2,1)S(1)} collective-permute-done((bf16[256,512]{1,0:T(8,128)(2,1)S(1)}, bf16[256,512]{1,0:T(8,128)(2,1)S(1)}, u32[]{:S(2)}, u32[]{:S(2)}) %collective-permute-start.1) | collective-permute-done | bytes 262176 | tf_op jit(solution)/shard_map/ppermute | solution.py:172
  35.0 0.0 collective-permute-done.2.other_ref
  35.0 6.6 %layer.1 = bf16[256,512]{1,0:T(8,128)(2,1)} custom-call(s32[10]{0:T(128)S(1)} %concatenate.12.meta_ref, bf16[256,512]{1,0:T(8,128)(2,1)S(1)} %collective-permute-done.near_ref, bf16[256,512]{1,0:T(8,128)(2,1)S(1)} %collective-permute-done.1.far_ref, bf16[16,8,1152]{2,1,0:T(8,128)(2,1)S(1)} %bitcast.6, ...), custom_call_target="tpu_custom_call" | custom-call | flops 1744830464 | bytes 4718592 | tf_op jit(solution)/shard_map/layer/pallas_call | solution.py:192
  (5 shorter events, 0.1 us)
Async XLA Ops:
  0.0 26.4 %copy-start.1 = (s32[2,2]{1,0:T(2,128)S(1)}, s32[2,2]{1,0:T(2,128)}, u32[]{:S(2)}) copy-start(s32[2,2]{1,0:T(2,128)} %param.12) | copy-start | bytes 52
  0.0 26.5 %copy-start = (s32[2]{0:T(128)S(1)}, s32[2]{0:T(128)}, u32[]{:S(2)}) copy-start(s32[2]{0:T(128)} %param.13) | copy-start | bytes 28
  2.1 10.6 %all-to-all-start = ((bf16[4,8,1152]{2,1,0:T(8,128)(2,1)}), bf16[4,8,1152]{2,1,0:T(8,128)(2,1)S(1)}, u32[]{:S(2)}, u32[]{:S(2)}) async-start(bf16[4,8,1152]{2,1,0:T(8,128)(2,1)} %broadcast_in_dim.4), calls=%async_computation | async-start | bytes 147456 | tf_op jit(solution)/shard_map/all_to_all | solution.py:157
  13.5 9.0 %all-to-all-start.1 = ((bf16[4,4,8,1152]{3,2,1,0:T(8,128)(2,1)}), bf16[4,4,8,1152]{3,2,1,0:T(8,128)(2,1)S(1)}, u32[]{:S(2)}, u32[]{:S(2)}) async-start(bf16[4,4,8,1152]{3,2,1,0:T(8,128)(2,1)} %broadcast_in_dim.5), calls=%async_computation.1 | async-start | bytes 589824 | tf_op jit(solution)/shard_map/all_to_all | solution.py:175
  22.5 12.5 %collective-permute-start.2 = (bf16[16,8,1152]{2,1,0:T(8,128)(2,1)S(1)}, bf16[16,8,1152]{2,1,0:T(8,128)(2,1)S(1)}, u32[]{:S(2)}, u32[]{:S(2)}) collective-permute-start(bf16[16,8,1152]{2,1,0:T(8,128)(2,1)S(1)} %bitcast.5), channel_id=1, source_target_pairs={{0,1},{1,0},{2,3},{3,2},{4,5},{5,4},{6,7},{7,6},{8,9},{9,8},{10,11... | collective-permute-start | bytes 884744 | tf_op jit(solution)/shard_map/ppermute | solution.py:178
  22.5 4.0 %collective-permute-start = (bf16[256,512]{1,0:T(8,128)(2,1)S(1)}, bf16[256,512]{1,0:T(8,128)(2,1)S(1)}, u32[]{:S(2)}, u32[]{:S(2)}) collective-permute-start(bf16[256,512]{1,0:T(8,128)(2,1)S(1)} %get-tuple-element.18), channel_id=1, source_target_pairs={{0,1},{1,0},{2,3},{3,2},{4,5},{5,4},{6,7},{7,6},{8,9},{9,8},{10,11... | collective-permute-start | bytes 786440 | tf_op jit(solution)/shard_map/ppermute | solution.py:173
  23.1 11.9 %collective-permute-start.1 = (bf16[256,512]{1,0:T(8,128)(2,1)S(1)}, bf16[256,512]{1,0:T(8,128)(2,1)S(1)}, u32[]{:S(2)}, u32[]{:S(2)}) collective-permute-start(bf16[256,512]{1,0:T(8,128)(2,1)S(1)} %get-tuple-element.17), channel_id=1, source_target_pairs={{1,2},{3,4},{5,6},{7,8},{9,10},{11,12},{13,14},{15,16},{17,18},{19... | collective-permute-start | bytes 786440 | tf_op jit(solution)/shard_map/ppermute | solution.py:172
